TPU v7x, 256 devices: a whole 4x4x8 slice. The times are simulated.
256 devices in a mesh: island: 16 (over z_lo, y), fsdp: 16 (over z_hi, x, core).
Axes of the slice: x: 4, y: 4, z: 8 (z_hi: 2, z_lo: 4; z = z_hi * 4 + z_lo), core: 2. Of those that a mesh axis runs over, the one named last changes fastest.
Arguments:
- tokens_in: bfloat16 [16, 2, 4096, 8192], P('island', None, 'fsdp'), may hold values from -6 to 6
- norm_gain: float32 [8192], replicated, may hold values from 0.1 to 1.9
- local_weights: float32 [16, 8192, 512], P('island', 'fsdp'), may hold values from -0.0625 to 0.0625
- cotangent: bfloat16 [16, 2, 4096, 512], P('island', None, 'fsdp'), may hold values from -6 to 6
- delta_levels: bfloat16 [16, 8192, 512], P('island', 'fsdp'), may hold values from -127 to 127, as said below
- block_scales: float32 [16, 8192, 4], P('island', 'fsdp'), may hold values from 5.5242715e-05 to 0.0002762136
- outer_weights_in: float32 [8192, 512], P('fsdp'), may hold values from -0.0625 to 0.0625
- momentum_in: float32 [8192, 512], P('fsdp'), may hold values from -0.03314563 to 0.03314563
Outputs:
- keys: bfloat16 [16, 2, 4096, 512], P('island', None, 'fsdp')
- merged: float32 [16, 8192, 512], P('island', 'fsdp')
- outer_weights: float32 [8192, 512], P('fsdp')
- outer_momentum: float32 [8192, 512], P('fsdp')
Inputs may be any that keep to these rules, and one draw needn't show every extreme that they name: `delta_levels`: whole numbers.
All inputs are finite; a program needn't handle non-finite values.
Results may differ from a plain program's by a relative error of at most 0.012.
Values may be sent and summed in bfloat16 or wider, within the bound.
A program may use at most 128 MiB of HBM per device.

v0:
```python
import math

import jax
import jax.numpy as jnp
from jax import lax
from jax.sharding import PartitionSpec as P

BLOCK = 128


norm_eps = 1e-05
inner_rate = 0.3
outer_rate = 0.7
keep_rate = 0.9
mix_share = 0.5


def normalize(activations, norm_gain):
    widened = activations.astype(jnp.float32)
    spread = jnp.mean(widened * widened, axis=-1, keepdims=True)
    return (widened * lax.rsqrt(spread + norm_eps) * norm_gain).astype(jnp.bfloat16)


def outer_update(summed, weights_part, momentum_part, islands):
    mean_delta = summed / islands
    new_momentum = keep_rate * momentum_part + mean_delta
    new_weights = weights_part - outer_rate * (mean_delta + keep_rate * new_momentum)
    return (new_weights, new_momentum)


def on_device(
    tokens_in,
    norm_gain,
    local_weights,
    cotangent,
    delta_levels,
    block_scales,
    outer_weights_in,
    momentum_in,
):
    features = tokens_in.shape[-1]
    scale_root = math.sqrt(features)
    groups = lax.axis_size("fsdp")
    normed = normalize(tokens_in[0].reshape(-1, features), norm_gain)
    local_rows = normed.shape[0]
    master = local_weights[0]
    key_width = master.shape[1]
    tangent = cotangent[0].reshape(local_rows, key_width)
    compute_weights = master.astype(jnp.bfloat16)
    col_block = normed
    projected = jnp.dot(
        col_block,
        lax.all_gather(compute_weights, "fsdp", axis=0, tiled=True),
        preferred_element_type=jnp.float32,
    )
    col_block = normed
    gradient = (
        lax.psum_scatter(
            jnp.einsum("td,tk->dk", col_block, tangent, preferred_element_type=jnp.float32).astype(
                jnp.bfloat16
            ),
            "fsdp",
            scatter_dimension=0,
            tiled=True,
        ).astype(jnp.float32)
        / scale_root
    )
    key_output = projected.astype(jnp.bfloat16).reshape(cotangent.shape)
    inner_weights = master - inner_rate * gradient / math.sqrt(local_rows * groups)
    dequantized = delta_levels[0].astype(jnp.float32) * jnp.repeat(block_scales[0], BLOCK, axis=1)
    islands = lax.axis_size("island")
    summed = lax.psum(dequantized.astype(jnp.bfloat16), "island").astype(jnp.float32)
    weights_new, momentum_new = outer_update(summed, outer_weights_in, momentum_in, islands)
    merged = mix_share * inner_weights + (1.0 - mix_share) * weights_new
    return (key_output, merged[None], weights_new, momentum_new)


def solution(mesh):
    in_specs = (
        P("island", None, "fsdp", None),
        P(),
        P("island", "fsdp", None),
        P("island", None, "fsdp", None),
        P("island", "fsdp", None),
        P("island", "fsdp", None),
        P("fsdp", None),
        P("fsdp", None),
    )
    out_specs = (
        P("island", None, "fsdp", None),
        P("island", "fsdp", None),
        P("fsdp", None),
        P("fsdp", None),
    )
    return jax.shard_map(
        on_device, mesh=mesh, in_specs=in_specs, out_specs=out_specs, check_vma=False
    )
```

profile of v0, /device:TPU:1, one launch (start us, length us, event | category | flops | bytes accessed | tf_op | source)
XLA Modules:
  0.0 297.9 jit_solution(2229693860785813865)
XLA Ops:
  8.0 0.0 copy-start
  8.0 0.0 copy-start.4
  8.0 0.0 all-reduce.2.cloned.1.call-start
  8.1 0.9 copy.13
  9.0 0.6 broadcast_in_dim.8
  9.6 2.0 fusion.7
  11.6 0.0 all-reduce.2.cloned.1.call-update
  11.6 0.0 reduce-scatter.2.cloned.1.call-start
  11.7 0.0 copy-start.1
  11.7 5.3 %multiply_reduce_fusion = f32[2,256]{1,0:T(2,128)S(1)} fusion(bf16[1,2,256,8192]{3,2,1,0:T(8,128)(2,1)} %param.8), kind=kLoop, calls=%fused_computation.5 | loop fusion | flops 12582400 | bytes 8390656 | tf_op jit(solution)/shard_map/reduce_sum | solution.py:20
  16.9 0.0 copy-done
  17.0 0.0 copy-done.4
  17.0 0.5 copy-done.1
  17.4 7.1 %bitcast_convert_fusion = bf16[8192,512]{1,0:T(8,128)(2,1)} fusion(bf16[1,2,256,8192]{3,2,1,0:T(8,128)(2,1)S(1)} %copy-done.1, f32[8192]{0:T(1024)S(1)} %copy-done.4, f32[2,256]{1,0:T(2,128)S(1)} %get-tuple-element.7, bf16[1,2,256,512]{3,2,1,0:T(8,128)(2,1)S(1)} %copy-done), kind=kOutput, calls=%fused_computation | convolution fusion | flops 4315938816 | bytes 17336320 | tf_op jit(solution)/shard_map/td,tk->dk/dot_general | solution.py:59
  24.5 0.0 copy-start.2
  24.5 0.0 reduce-scatter.2.cloned.1.call-update
  24.6 0.0 all-gather.2.cloned.1.call-start
  24.6 1.1 copy-done.2
  25.8 0.9 bitcast_convert_fusion.1
  26.6 0.0 all-gather.2.cloned.1.call-update
  26.7 0.0 copy-start.3
  26.7 9.9 %fusion.1 = bf16[512,8192]{1,0:T(8,128)(2,1)} fusion(bf16[1,2,256,8192]{3,2,1,0:T(8,128)(2,1)} %param.8, f32[8192]{0:T(1024)S(1)} %copy-done.4, f32[512]{0:T(512)S(1)} %bitcast.41), kind=kLoop, calls=%fused_computation.3 | loop fusion | flops 16777216 | bytes 16812032 | tf_op jit(solution)/shard_map/convert_element_type | solution.py:21
  36.6 172.2 %all-reduce.2.cloned.1.call-done = bf16[512,512]{1,0:T(8,128)(2,1)} async-done(((bf16[512,512]{1,0:T(8,128)(2,1)}), bf16[512,512]{1,0:T(8,128)(2,1)}) %all-reduce.2.cloned.1.call-update) | async-done | bytes 524304 | tf_op jit(solution)/shard_map/psum | solution.py:72
  208.9 0.0 reduce-scatter.2.cloned.1.call-done
  208.9 0.0 copy-done.3
  208.9 3.6 %fusion.10 = (f32[1,512,512]{2,1,0:T(8,128)}, f32[512,512]{1,0:T(8,128)}, f32[512,512]{1,0:T(8,128)}) fusion(f32[1,512,512]{2,1,0:T(8,128)S(1)} %copy-done.2, bf16[512,512]{1,0:T(8,128)(2,1)} %reduce-scatter.2.cloned.1.call-done, f32[512,512]{1,0:T(8,128)S(1)} %copy-done.3, bf16[512,512]{1,0:T(8,128)(2,1)} %all-reduce.2.cloned.1.call-done, f32[512,512]{1,0:T(8,128)} %param.15), kind=kLoop, calls=%fused_computation.17 | loop fusion | flops 3407872 | bytes 7340032 | tf_op jit(solution)/shard_map/broadcast_in_dim | solution.py:75
  212.5 66.9 %all-gather.2.cloned.1.call-done = bf16[8192,512]{1,0:T(8,128)(2,1)} async-done(((bf16[512,512]{1,0:T(8,128)(2,1)}), bf16[8192,512]{1,0:T(8,128)(2,1)}) %all-gather.2.cloned.1.call-update) | async-done | bytes 8388624 | tf_op jit(solution)/shard_map/all_gather | solution.py:53
  279.4 11.0 %convolution_convert_fusion = bf16[512,512]{1,0:T(8,128)(2,1)} fusion(bf16[512,8192]{1,0:T(8,128)(2,1)} %fusion.1, bf16[8192,512]{1,0:T(8,128)(2,1)} %all-gather.2.cloned.1.call-done), kind=kOutput, calls=%fused_computation.10 | convolution fusion | flops 4295229440 | bytes 17301504 | tf_op jit(solution)/shard_map/dot_general | solution.py:51
  (2 shorter events, 0.0 us)
Async XLA Ops:
  8.0 9.0 %copy-start = (bf16[1,2,256,512]{3,2,1,0:T(8,128)(2,1)S(1)}, bf16[1,2,256,512]{3,2,1,0:T(8,128)(2,1)}, u32[]{:S(2)}) copy-start(bf16[1,2,256,512]{3,2,1,0:T(8,128)(2,1)} %param.11) | copy-start | bytes 1572868
  8.0 8.9 %copy-start.4 = (f32[8192]{0:T(1024)S(1)}, f32[8192]{0:T(1024)}, u32[]{:S(2)}) copy-start(f32[8192]{0:T(1024)} %param.9) | copy-start | bytes 98308
  8.0 200.8 %all-reduce.2.cloned.1.call-start = ((), (), s32[]{:S(2)}) async-start(), calls=%async_computation.3 | async-start | bytes 1048576 | tf_op jit(solution)/shard_map/psum | solution.py:72
  11.6 197.2 %reduce-scatter.2.cloned.1.call-start = ((), (), s32[]{:S(2)}) async-start(), calls=%async_computation.2 | async-start | bytes 8912896 | tf_op jit(solution)/shard_map/reduce_scatter | solution.py:58
  11.7 5.8 %copy-start.1 = (bf16[1,2,256,8192]{3,2,1,0:T(8,128)(2,1)S(1)}, bf16[1,2,256,8192]{3,2,1,0:T(8,128)(2,1)}, u32[]{:S(2)}) copy-start(bf16[1,2,256,8192]{3,2,1,0:T(8,128)(2,1)} %param.8) | copy-start | bytes 25165828
  24.5 1.2 copy-start.2
  24.6 254.8 %all-gather.2.cloned.1.call-start = ((), (), s32[]{:S(2)}) async-start(), calls=%async_computation.1 | async-start | bytes 8912896 | tf_op jit(solution)/shard_map/all_gather | solution.py:53
  26.7 182.2 %copy-start.3 = (f32[512,512]{1,0:T(8,128)S(1)}, f32[512,512]{1,0:T(8,128)}, u32[]{:S(2)}) copy-start(f32[512,512]{1,0:T(8,128)} %param.14) | copy-start | bytes 3145732
Sparse Core Ops, SparseCore 0:
  12.0 196.7 all-reduce.1
Sparse Core Ops, SparseCore 1:
  24.6 141.0 reduce-scatter.1
  168.9 110.4 all-gather.1
where the time goes:
time: 298 us
  waiting for transfers between devices  239 us (80%)
  other arithmetic  21.7 us (7%)
  matrix products  18.1 us (6%)
  between operations  15.5 us (5%)
  local copies, waits for them, and re-layouts  3.14 us (1%)
    psum x1, waiting for transfers between devices, on_device(): lax.psum(dequantized.astype(jnp.bfloat16), 'island').astype(jnp.float32)  172 us
    all_gather x1, waiting for transfers between devices, on_device(): lax.all_gather(compute_weights, 'fsdp', axis=0, tiled=True)  66.9 us
    dot_general x1, matrix products, on_device(): jnp.dot(col_block, lax.all_gather(compute_weights, 'fsdp', axis=0, tiled=...  11 us
    convert_element_type x1, other arithmetic, normalize(): (widened * lax.rsqrt(spread + norm_eps) * norm_gain).astype(jnp.bfloat16)  9.95 us
    dot_general x1, matrix products, on_device(): jnp.einsum('td,tk->dk', col_block, tangent, preferred_element_type=jnp.fl...  7.09 us
  transfers between devices with their start and end apart: 3, of which 2 were waited for; matrix products, arithmetic and copies ran while one was open for 9% of the time, Pallas kernels for 0%

commit v1 on v0

v1 whole, which is shorter than its diff:
```python
import functools
import math

import jax
import jax.numpy as jnp
from jax import lax
from jax.experimental import pallas as pl
from jax.experimental.pallas import tpu as pltpu
from jax.sharding import PartitionSpec as P

BLOCK = 128
NX = 4
NY = 4
NZ = 4
ROWS = 512
KV = 512
D = 8192
HALF = 256
QUARTER = 128
CHUNK = 64

norm_eps = 1e-05
inner_rate = 0.3
outer_rate = 0.7
keep_rate = 0.9
mix_share = 0.5

MESH = pl.DeviceIdType.MESH
f32 = jnp.float32
bf16 = jnp.bfloat16


def kernel(
    step_scale,
    tok_hbm,
    gain,
    w_hbm,
    cot_hbm,
    lev_hbm,
    scales,
    keys_out,
    inner_out,
    sum_out,
    tok,
    wf,
    cot,
    lev,
    wg,
    acc,
    p_out,
    p_in,
    q,
    r_a,
    r_b,
    from_m,
    from_p,
    z_out,
    z_in,
    y_in,
    zl_in,
    load_sem,
    send_sem,
    recv_sem,
):
    f = lax.axis_index("fsdp")
    i = lax.axis_index("island")
    zh, x, c = f // 8, (f // 2) % NX, f % 2
    zl, y = i // NY, i % NY

    def fs(dz, dx, dc):
        return ((zh + dz) % 2) * 8 + ((x + dx) % NX) * 2 + (c + dc) % 2

    def to_fsdp(dz, dx, dc):
        return {"fsdp": fs(dz, dx, dc), "island": i}

    def to_island(dzl, dy):
        return {"fsdp": f, "island": ((zl + dzl) % NZ) * NY + (y + dy) % NY}

    right, left = to_fsdp(0, 1, 0), to_fsdp(0, NX - 1, 0)
    across, other = to_fsdp(1, 0, 0), to_fsdp(0, 0, 1)

    started = []

    def remote(k, src, dst, device):
        return pltpu.make_async_remote_copy(
            src_ref=src,
            dst_ref=dst,
            send_sem=send_sem.at[k],
            recv_sem=recv_sem.at[k],
            device_id=device,
            device_id_type=MESH,
        )

    counter = [0]

    def role(src, dst, device):
        copy = remote(counter[0], src, dst, device)
        counter[0] += 1
        started.append(copy)
        return copy

    load_w = pltpu.make_async_copy(w_hbm, wf, load_sem.at[0])
    load_w.start()
    load_lev = pltpu.make_async_copy(lev_hbm, lev, load_sem.at[1])
    load_lev.start()
    loads = []
    for n in range(ROWS // CHUNK):
        rows = pl.ds(n * CHUNK, CHUNK)
        load = pltpu.make_async_copy(tok_hbm.at[rows], tok.at[rows], load_sem.at[3 + n])
        load.start()
        loads.append(load)
    load_cot = pltpu.make_async_copy(cot_hbm, cot, load_sem.at[2])
    load_cot.start()

    barrier = pltpu.get_barrier_semaphore()
    peers = [right, left, across, other]
    peers += [to_island(0, d) for d in (1, 2, 3)] + [to_island(d, 0) for d in (1, 2, 3)]
    for peer in peers:
        pl.semaphore_signal(barrier, inc=1, device_id=peer, device_id_type=MESH)
    load_w.wait()
    wg[0, 0, 0] = wf[...].astype(bf16)
    pl.semaphore_wait(barrier, len(peers))

    def quarter(n):
        return pl.ds(n * QUARTER, QUARTER)

    ag_right, ag_left, ag_relay, ag_other = {}, {}, {}, {}
    for zz in range(2):
        for n in (0, 1, 2, 3):
            rows = quarter(n)
            ag_right[zz, n] = role(wg.at[zz, 0, 0, rows], wg.at[zz, 3, 0, rows], right)
        for n in (1, 0, 3, 2):
            rows = quarter(n)
            ag_left[zz, n] = role(wg.at[zz, 0, 0, rows], wg.at[zz, 1, 0, rows], left)
        for n in (0, 2):
            rows = quarter(n)
            ag_relay[zz, n] = role(wg.at[zz, 3, 0, rows], wg.at[zz, 2, 0, rows], right)
        for n in (1, 3):
            rows = quarter(n)
            ag_relay[zz, n] = role(wg.at[zz, 1, 0, rows], wg.at[zz, 2, 0, rows], left)
        for dx in range(4):
            ag_other[zz, dx] = role(wg.at[zz, dx, 0], wg.at[zz, dx, 1], other)
    ag_z = [role(wg.at[0, 0, 0, quarter(n)], wg.at[1, 0, 0, quarter(n)], across) for n in range(4)]

    low, high = pl.ds(0, HALF), pl.ds(HALF, HALF)
    opp_left, opp_right, dir_right, dir_left, sum_right, sum_left = {}, {}, {}, {}, {}, {}
    for zz in range(2):
        opp_left[zz] = role(q.at[zz, 2, low], r_a.at[zz], left)
        opp_right[zz] = role(q.at[zz, 2, high], r_b.at[zz], right)
        dir_right[zz] = role(q.at[zz, 1, low], from_m.at[zz, low], right)
        dir_left[zz] = role(q.at[zz, 3, high], from_p.at[zz, high], left)
        for n in range(2):
            rows = pl.ds(HALF + n * QUARTER, QUARTER)
            sum_right[zz, n] = role(q.at[zz, 1, rows], from_m.at[zz, rows], right)
            rows = pl.ds(n * QUARTER, QUARTER)
            sum_left[zz, n] = role(q.at[zz, 3, rows], from_p.at[zz, rows], left)
    z_send = [role(z_out.at[quarter(n)], z_in.at[quarter(n)], across) for n in range(4)]

    y_part = []
    for d in (1, 2, 3):
        rows = pl.ds(pl.multiple_of(((y + d) % NY) * QUARTER, QUARTER), QUARTER)
        y_part.append(role(lev.at[rows], y_in.at[d - 1], to_island(0, d)))
    zl_part = [role(zl_in.at[zl], zl_in.at[zl], to_island(d, 0)) for d in (1, 2, 3)]
    mine = pl.ds(pl.multiple_of(y * QUARTER, QUARTER), QUARTER)
    y_sum = [role(sum_out.at[mine], sum_out.at[mine], to_island(0, d)) for d in (1, 2, 3)]

    base = counter[0]

    def pair(zz, dx):
        return remote(base + zz * 4 + dx, p_out.at[zz, dx], p_in.at[zz, dx], other)

    for n in range(2):
        for m in range(2):
            ag_right[0, 2 * n + m].start()
            ag_left[0, 2 * n + 1 - m].start()
        ag_z[2 * n].start()
        ag_z[2 * n + 1].start()
    ag_other[0, 0].start()

    load_lev.wait()
    for b in range(KV // BLOCK):
        cols = pl.ds(b * BLOCK, BLOCK)
        lev[:, cols] = (lev[:, cols].astype(f32) * scales[:, b : b + 1]).astype(bf16)
    for copy in y_part:
        copy.start()

    def normalize(first):
        def body(n, carry):
            rows = pl.ds(pl.multiple_of(first + n * 16, 16), 16)
            total = jnp.zeros((16, 128), f32)
            for k in range(D // 128):
                v = tok[rows, k * 128 : (k + 1) * 128].astype(f32)
                total += v * v
            spread = jnp.sum(total, axis=1, keepdims=True) / D
            inv = lax.rsqrt(spread + norm_eps)
            for k in range(D // 128):
                cols = pl.ds(k * 128, 128)
                v = tok[rows, cols].astype(f32)
                tok[rows, cols] = (v * inv * gain[:, cols]).astype(bf16)
            return carry

        lax.fori_loop(0, CHUNK // 16, body, 0)

    for n in range(ROWS // CHUNK):
        loads[n].wait()
        normalize(n * CHUNK)
        if n == 3:
            ag_right[0, 0].wait_recv()
            ag_relay[0, 0].start()
            ag_left[0, 1].wait_recv()
            ag_relay[0, 1].start()

    def columns(dz, dx, dc):
        return pl.ds(pl.multiple_of(fs(dz, dx, dc) * ROWS, ROWS), ROWS)

    def gradient(dz, dx, dc):
        return lax.dot_general(
            tok[:, columns(dz, dx, dc)],
            cot[...],
            (((0,), (0,)), ((), ())),
            preferred_element_type=f32,
        )

    def gradients(zz):
        def give(n, carry):
            dx = (2 + n) % 4
            p_out[zz, dx] = gradient(zz, dx, 1).astype(bf16)
            pair(zz, dx).start()
            return carry

        lax.fori_loop(0, 4, give, 0)

        def keep(n, carry):
            dx = (2 + n) % 4
            pair(zz, dx).wait_recv()
            q[zz, dx] = (gradient(zz, dx, 0) + p_in[zz, dx].astype(f32)).astype(bf16)
            return carry

        lax.fori_loop(0, 4, keep, 0)

    def scatter(zz):
        opp_left[zz].start()
        opp_right[zz].start()
        dir_right[zz].start()
        dir_left[zz].start()

    def scatter_sums(zz):
        opp_right[zz].wait_recv()
        q[zz, 1, high] = (q[zz, 1, high].astype(f32) + r_b[zz].astype(f32)).astype(bf16)
        for n in range(2):
            sum_right[zz, n].start()
        opp_left[zz].wait_recv()
        q[zz, 3, low] = (q[zz, 3, low].astype(f32) + r_a[zz].astype(f32)).astype(bf16)
        for n in range(2):
            sum_left[zz, n].start()

    def key_block(zz, dx, dc):
        return jnp.dot(tok[:, columns(zz, dx, dc)], wg[zz, dx, dc], preferred_element_type=f32)

    def key_pair(zz, dx, first=False):
        ag_other[zz, dx].wait_recv()

        def body(dc, carry):
            acc[...] += key_block(zz, dx, dc)
            return carry

        if first:
            acc[...] = jnp.zeros_like(acc)
        lax.fori_loop(0, 2, body, 0)

    def relay(zz, n):
        (ag_right if n % 2 == 0 else ag_left)[zz, n].wait_recv()
        ag_relay[zz, n].start()

    relay(0, 2)
    relay(0, 3)
    load_cot.wait()
    gradients(1)
    scatter(1)

    for copy in y_part:
        copy.wait_recv()
    part = lev[mine].astype(f32)
    for d in range(3):
        part += y_in[d].astype(f32)
    zl_in[zl] = part.astype(bf16)
    for copy in zl_part:
        copy.start()

    for n in (1, 3):
        ag_right[0, n].wait_recv()
    ag_other[0, 3].start()
    for n in (0, 2):
        ag_left[0, n].wait_recv()
    ag_other[0, 1].start()
    key_pair(0, 0, first=True)
    for n in range(4):
        ag_relay[0, n].wait_recv()
    ag_other[0, 2].start()

    for n in range(4):
        ag_z[n].wait_recv()
    gradients(0)
    scatter_sums(1)
    for n in range(2):
        for m in range(2):
            ag_right[1, 2 * n + m].start()
            ag_left[1, 2 * n + 1 - m].start()
    ag_other[1, 0].start()

    for copy in zl_part:
        copy.wait_recv()
    whole = zl_in[0].astype(f32)
    for d in range(1, NZ):
        whole += zl_in[d].astype(f32)
    sum_out[mine] = whole.astype(bf16)
    for copy in y_sum:
        copy.start()

    key_pair(0, 3)
    key_pair(0, 1)
    key_pair(0, 2)
    key_pair(1, 0)

    dir_right[1].wait_recv()
    dir_left[1].wait_recv()
    for n in range(2):
        sum_left[1, n].wait_recv()
        sum_right[1, n].wait_recv()
    z_out[...] = (q[1, 0].astype(f32) + from_m[1].astype(f32) + from_p[1].astype(f32)).astype(bf16)
    for n in range(4):
        z_send[n].start()

    for n in range(4):
        relay(1, n)
    scatter(0)
    for n in (1, 3):
        ag_right[1, n].wait_recv()
    ag_other[1, 3].start()
    for n in (0, 2):
        ag_left[1, n].wait_recv()
    ag_other[1, 1].start()
    key_pair(1, 3)
    key_pair(1, 1)
    scatter_sums(0)
    for n in range(4):
        ag_relay[1, n].wait_recv()
    ag_other[1, 2].start()
    key_pair(1, 2)
    keys_out[...] = acc[...].astype(bf16)

    for copy in y_sum:
        copy.wait_recv()
    for n in range(4):
        z_send[n].wait_recv()
    dir_right[0].wait_recv()
    dir_left[0].wait_recv()

    def finish(n):
        rows = quarter(n)
        total = q[0, 0, rows].astype(f32) + z_in[rows].astype(f32)
        total += from_m[0, rows].astype(f32) + from_p[0, rows].astype(f32)
        inner_out[rows] = wf[rows] - step_scale * total

    sum_left[0, 0].wait_recv()
    finish(0)
    sum_right[0, 0].wait_recv()
    finish(2)
    sum_left[0, 1].wait_recv()
    finish(1)
    sum_right[0, 1].wait_recv()
    finish(3)
    for copy in started:
        copy.wait_send()

    def drain(n, carry):
        pair(n // 4, n % 4).wait_send()
        return carry

    lax.fori_loop(0, 8, drain, 0)


N_ROLES = 160


def on_device(
    tokens_in,
    norm_gain,
    local_weights,
    cotangent,
    delta_levels,
    block_scales,
    outer_weights_in,
    momentum_in,
):
    features = tokens_in.shape[-1]
    groups = lax.axis_size("fsdp")
    islands = lax.axis_size("island")
    tokens = tokens_in[0].reshape(-1, features)
    tangent = cotangent[0].reshape(-1, cotangent.shape[-1])
    local_rows = tokens.shape[0]
    step_scale = inner_rate / math.sqrt(features) / math.sqrt(local_rows * groups)

    any_space = pl.BlockSpec(memory_space=pl.ANY)
    vmem = pl.BlockSpec(memory_space=pltpu.VMEM)
    keys, inner_weights, summed = pl.pallas_call(
        functools.partial(kernel, step_scale),
        out_shape=(
            jax.ShapeDtypeStruct((ROWS, KV), bf16),
            jax.ShapeDtypeStruct((ROWS, KV), f32),
            jax.ShapeDtypeStruct((ROWS, KV), bf16),
        ),
        in_specs=[any_space, vmem, any_space, any_space, any_space, vmem],
        out_specs=(vmem, vmem, vmem),
        scratch_shapes=[
            pltpu.VMEM((ROWS, D), bf16),
            pltpu.VMEM((ROWS, KV), f32),
            pltpu.VMEM((ROWS, KV), bf16),
            pltpu.VMEM((ROWS, KV), bf16),
            pltpu.VMEM((2, 4, 2, ROWS, KV), bf16),
            pltpu.VMEM((ROWS, KV), f32),
            pltpu.VMEM((2, 4, ROWS, KV), bf16),
            pltpu.VMEM((2, 4, ROWS, KV), bf16),
            pltpu.VMEM((2, 4, ROWS, KV), bf16),
            pltpu.VMEM((2, HALF, KV), bf16),
            pltpu.VMEM((2, HALF, KV), bf16),
            pltpu.VMEM((2, ROWS, KV), bf16),
            pltpu.VMEM((2, ROWS, KV), bf16),
            pltpu.VMEM((ROWS, KV), bf16),
            pltpu.VMEM((ROWS, KV), bf16),
            pltpu.VMEM((3, QUARTER, KV), bf16),
            pltpu.VMEM((NZ, QUARTER, KV), bf16),
            pltpu.SemaphoreType.DMA((3 + ROWS // CHUNK,)),
            pltpu.SemaphoreType.DMA((N_ROLES,)),
            pltpu.SemaphoreType.DMA((N_ROLES,)),
        ],
        compiler_params=pltpu.CompilerParams(
            collective_id=0, has_side_effects=True, vmem_limit_bytes=50 * 2**20
        ),
        cost_estimate=pl.CostEstimate(
            flops=4 * ROWS * D * KV, bytes_accessed=14 * 2**20, transcendentals=ROWS
        ),
    )(
        tokens,
        norm_gain.reshape(1, -1),
        local_weights[0],
        tangent,
        delta_levels[0],
        block_scales[0],
    )
    mean_delta = summed.astype(f32) / islands
    momentum_new = keep_rate * momentum_in + mean_delta
    weights_new = outer_weights_in - outer_rate * (mean_delta + keep_rate * momentum_new)
    merged = mix_share * inner_weights + (1.0 - mix_share) * weights_new
    return (keys.reshape(cotangent.shape), merged[None], weights_new, momentum_new)


def solution(mesh):
    in_specs = (
        P("island", None, "fsdp", None),
        P(),
        P("island", "fsdp", None),
        P("island", None, "fsdp", None),
        P("island", "fsdp", None),
        P("island", "fsdp", None),
        P("fsdp", None),
        P("fsdp", None),
    )
    out_specs = (
        P("island", None, "fsdp", None),
        P("island", "fsdp", None),
        P("fsdp", None),
        P("fsdp", None),
    )
    return jax.shard_map(
        on_device, mesh=mesh, in_specs=in_specs, out_specs=out_specs, check_vma=False
    )
```

time: 298 us -> 94.2 us (0.32)
  waiting for transfers between devices: 239 us -> 0 us
  Pallas kernels: 0 us -> 85.6 us
  other arithmetic: 21.7 us -> 2.07 us
  matrix products: 18.1 us -> 0 us
  between operations: 15.5 us -> 0.67 us
    psum x1 -> x0, waiting for transfers between devices: 172 us -> none  [on_device(): lax.psum(dequantized.astype(jnp.bfloat16), 'island').astype(jnp.float32)]
    pallas_call x0 -> x1, Pallas kernels: none -> 85.6 us  [on_device(): pl.pallas_call(functools.partial(kernel, step_scale), out_shape=(jax.Shap...]
    all_gather x1 -> x0, waiting for transfers between devices: 66.9 us -> none  [on_device(): lax.all_gather(compute_weights, 'fsdp', axis=0, tiled=True)]
    dot_general x2 -> x0, matrix products: 18.1 us -> none  [the longest x1 11 us: on_device(): jnp.dot(col_block, lax.all_gather(compute_weights, 'fsdp', axis=0, tiled=...]
    convert_element_type x3 -> x0, other arithmetic: 12.8 us -> none  [the longest x1 9.95 us: normalize(): (widened * lax.rsqrt(spread + norm_eps) * norm_gain).astype(jnp.bfloat16)]
    reduce_sum x1 -> x0, other arithmetic: 5.25 us -> none  [normalize(): spread = jnp.mean(widened * widened, axis=-1, keepdims=True)]
  transfers between devices with their start and end apart: 3 -> 0, of which waited for: 2 -> 0; matrix products, arithmetic and copies ran while one was open for 9% -> 0% of each run, Pallas kernels for 0% -> 0%
where the time goes in v1:
time: 94.2 us; the launch traced here: 92.9 us
  Pallas kernels  85.6 us (91%)
  local copies, waits for them, and re-layouts  4.47 us (5%)
  other arithmetic  2.07 us (2%)
    pallas_call x1, Pallas kernels, on_device(): pl.pallas_call(functools.partial(kernel, step_scale), out_shape=(jax.Shap...  85.6 us
    unnamed x12, local copies, waits for them, and re-layouts  4.47 us
    broadcast_in_dim x1, other arithmetic, on_device(): merged[None]  2.07 us

profile of v1, /device:TPU:1, one launch (start us, length us, event | category | flops | bytes accessed | tf_op | source)
XLA Modules:
  0.0 92.9 jit_solution(15072136800721913822)
XLA Ops:
  0.6 0.8 copy.12
  1.5 0.0 copy-start
  1.5 1.0 %copy-done = bf16[1,2,256,512]{3,2,1,0:T(8,128)(2,1)S(1)} copy-done((bf16[1,2,256,512]{3,2,1,0:T(8,128)(2,1)S(1)}, bf16[1,2,256,512]{3,2,1,0:T(8,128)(2,1)}, u32[]{:S(2)}) %copy-start) | copy-done | bytes 524312
  2.5 0.0 copy-start.1
  2.5 1.0 %copy-done.1 = bf16[1,512,512]{2,1,0:T(8,128)(2,1)S(1)} copy-done((bf16[1,512,512]{2,1,0:T(8,128)(2,1)S(1)}, bf16[1,512,512]{2,1,0:T(8,128)(2,1)}, u32[]{:S(2)}) %copy-start.1) | copy-done | bytes 524312
  3.6 0.0 copy-start.2
  3.6 0.8 copy-done.2
  4.3 0.0 copy-start.3
  4.3 0.0 copy-start.4
  4.3 85.6 %shard_map.111 = (bf16[512,512]{1,0:T(8,128)(2,1)S(1)}, f32[512,512]{1,0:T(8,128)S(1)}, bf16[512,512]{1,0:T(8,128)(2,1)S(1)}) custom-call(bf16[512,8192]{1,0:T(8,128)(2,1)} %bitcast.14, f32[1,8192]{1,0:T(1,128)S(1)} %bitcast.13, f32[512,512]{1,0:T(8,128)} %bitcast.15, bf16[512,512]{1,0:T(8,128)(2,1)S(1)} %bitcast.11, bf16[512,512]{1,0:T(8,128)(2,1)S(1)} %bitcast.12, ...), custom_call_target="tpu_custom_call" | custom-call | flops 8589934592 | bytes 14680064 | tf_op jit(solution)/shard_map/pallas_call | solution.py:406
  90.0 0.0 copy-done.3
  90.0 0.0 copy-done.4
  90.0 2.1 %multiply_bitcast_fusion = (f32[1,512,512]{2,1,0:T(8,128)}, f32[512,512]{1,0:T(8,128)}, f32[512,512]{1,0:T(8,128)}) fusion(f32[512,512]{1,0:T(8,128)S(1)} %get-tuple-element.8, f32[512,512]{1,0:T(8,128)S(1)} %copy-done.3, bf16[512,512]{1,0:T(8,128)(2,1)S(1)} %get-tuple-element.9, f32[512,512]{1,0:T(8,128)S(1)} %copy-done.4), kind=kLoop, calls=%fused_computation | loop fusion | flops 2621440 | bytes 6815744 | tf_op jit(solution)/shard_map/broadcast_in_dim | solution.py:455
  92.1 0.8 copy.14
Async XLA Ops:
  1.5 1.0 %copy-start = (bf16[1,2,256,512]{3,2,1,0:T(8,128)(2,1)S(1)}, bf16[1,2,256,512]{3,2,1,0:T(8,128)(2,1)}, u32[]{:S(2)}) copy-start(bf16[1,2,256,512]{3,2,1,0:T(8,128)(2,1)} %param.11) | copy-start | bytes 1572868
  2.5 1.0 %copy-start.1 = (bf16[1,512,512]{2,1,0:T(8,128)(2,1)S(1)}, bf16[1,512,512]{2,1,0:T(8,128)(2,1)}, u32[]{:S(2)}) copy-start(bf16[1,512,512]{2,1,0:T(8,128)(2,1)} %param.12) | copy-start | bytes 1572868
  3.6 0.8 copy-start.2
  4.3 85.7 %copy-start.3 = (f32[512,512]{1,0:T(8,128)S(1)}, f32[512,512]{1,0:T(8,128)}, u32[]{:S(2)}) copy-start(f32[512,512]{1,0:T(8,128)} %param.14) | copy-start | bytes 3145732
  4.3 85.7 %copy-start.4 = (f32[512,512]{1,0:T(8,128)S(1)}, f32[512,512]{1,0:T(8,128)}, u32[]{:S(2)}) copy-start(f32[512,512]{1,0:T(8,128)} %param.15) | copy-start | bytes 3145732

commit v2 on v1

v2 whole, which is shorter than its diff:
```python
import functools
import math

import jax
import jax.numpy as jnp
from jax import lax
from jax.experimental import pallas as pl
from jax.experimental.pallas import tpu as pltpu
from jax.sharding import PartitionSpec as P

BLOCK = 128
NX = 4
NY = 4
NZ = 4
ROWS = 512
KV = 512
D = 8192
HALF = 256
QUARTER = 128
PART = 32
CHUNK = 64

norm_eps = 1e-05
inner_rate = 0.3
outer_rate = 0.7
keep_rate = 0.9
mix_share = 0.5

MESH = pl.DeviceIdType.MESH
f32 = jnp.float32
bf16 = jnp.bfloat16


def kernel(
    step_scale,
    islands,
    tok_hbm,
    gain_hbm,
    w_hbm,
    cot_hbm,
    lev_hbm,
    scales_hbm,
    ow_hbm,
    mom_hbm,
    keys_out,
    merged_out,
    ow_out,
    mom_out,
    tok,
    gain,
    wf,
    cot,
    lev,
    scales,
    wg,
    acc,
    p_out,
    p_in,
    q,
    r_a,
    r_b,
    from_m,
    from_p,
    z_out,
    z_in,
    y_in,
    zl_out,
    zl_in,
    total_delta,
    load_sem,
    send_sem,
    recv_sem,
):
    f = lax.axis_index("fsdp")
    i = lax.axis_index("island")
    zh, x, c = f // 8, (f // 2) % NX, f % 2
    zl, y = i // NY, i % NY

    def fs(dz, dx, dc):
        return ((zh + dz) % 2) * 8 + ((x + dx) % NX) * 2 + (c + dc) % 2

    def to_fsdp(dz, dx, dc):
        return {"fsdp": fs(dz, dx, dc), "island": i}

    def to_island(dzl, dy):
        return {"fsdp": f, "island": ((zl + dzl) % NZ) * NY + (y + dy) % NY}

    right, left = to_fsdp(0, 1, 0), to_fsdp(0, NX - 1, 0)
    across, other = to_fsdp(1, 0, 0), to_fsdp(0, 0, 1)

    started = []
    counter = [0]

    def remote(k, src, dst, device):
        return pltpu.make_async_remote_copy(
            src_ref=src,
            dst_ref=dst,
            send_sem=send_sem.at[k],
            recv_sem=recv_sem.at[k],
            device_id=device,
            device_id_type=MESH,
        )

    def role(src, dst, device):
        copy = remote(counter[0], src, dst, device)
        counter[0] += 1
        started.append(copy)
        return copy

    load_count = [0]

    def load(src, dst):
        copy = pltpu.make_async_copy(src, dst, load_sem.at[load_count[0]])
        load_count[0] += 1
        copy.start()
        return copy

    load_w = load(w_hbm, wf)
    load_lev = load(lev_hbm, lev)
    load_scales = load(scales_hbm, scales)
    load_gain = load(gain_hbm, gain)
    loads = []
    for n in range(ROWS // CHUNK):
        rows = pl.ds(n * CHUNK, CHUNK)
        loads.append(load(tok_hbm.at[rows], tok.at[rows]))
    load_cot = load(cot_hbm, cot)
    load_ow = load(ow_hbm, ow_out)
    load_mom = load(mom_hbm, mom_out)

    barrier = pltpu.get_barrier_semaphore()
    peers = [right, left, across, other]
    peers += [to_island(0, d) for d in (1, 2, 3)] + [to_island(d, 0) for d in (1, 2, 3)]
    for peer in peers:
        pl.semaphore_signal(barrier, inc=1, device_id=peer, device_id_type=MESH)
    load_w.wait()
    wg[0, 0, 0] = wf[...].astype(bf16)
    pl.semaphore_wait(barrier, len(peers))

    def quarter(n):
        return pl.ds(n * QUARTER, QUARTER)

    ag_right, ag_left, ag_relay, ag_other = {}, {}, {}, {}
    for zz in range(2):
        for n in (0, 1, 2, 3):
            rows = quarter(n)
            ag_right[zz, n] = role(wg.at[zz, 0, 0, rows], wg.at[zz, 3, 0, rows], right)
        for n in (1, 0, 3, 2):
            rows = quarter(n)
            ag_left[zz, n] = role(wg.at[zz, 0, 0, rows], wg.at[zz, 1, 0, rows], left)
        for n in (0, 2):
            rows = quarter(n)
            ag_relay[zz, n] = role(wg.at[zz, 3, 0, rows], wg.at[zz, 2, 0, rows], right)
        for n in (1, 3):
            rows = quarter(n)
            ag_relay[zz, n] = role(wg.at[zz, 1, 0, rows], wg.at[zz, 2, 0, rows], left)
        for dx in range(4):
            ag_other[zz, dx] = role(wg.at[zz, dx, 0], wg.at[zz, dx, 1], other)
    ag_z = [role(wg.at[0, 0, 0, quarter(n)], wg.at[1, 0, 0, quarter(n)], across) for n in range(4)]

    low, high = pl.ds(0, HALF), pl.ds(HALF, HALF)
    opp_left, opp_right, dir_right, dir_left, sum_right, sum_left = {}, {}, {}, {}, {}, {}
    for zz in range(2):
        for n in range(2):
            part, upper, lower = quarter(n), quarter(n), quarter(2 + n)
            opp_left[zz, n] = role(q.at[zz, 2, upper], r_a.at[zz, part], left)
            opp_right[zz, n] = role(q.at[zz, 2, lower], r_b.at[zz, part], right)
            sum_left[zz, n] = role(q.at[zz, 3, upper], from_p.at[zz, upper], left)
            sum_right[zz, n] = role(q.at[zz, 1, lower], from_m.at[zz, lower], right)
        dir_right[zz] = role(q.at[zz, 1, low], from_m.at[zz, low], right)
        dir_left[zz] = role(q.at[zz, 3, high], from_p.at[zz, high], left)
    z_send = [role(z_out.at[quarter(n)], z_in.at[quarter(n)], across) for n in range(4)]

    def y_rows(d):
        return pl.ds(pl.multiple_of(((y + d) % NY) * QUARTER, QUARTER), QUARTER)

    def z_rows(d):
        return pl.ds(pl.multiple_of(((zl + d) % NZ) * PART, PART), PART)

    mine = y_rows(0)
    my_part = pl.ds(pl.multiple_of(y * QUARTER + zl * PART, PART), PART)
    steps = (1, 2, 3)
    y_part = [role(lev.at[y_rows(d)], y_in.at[d - 1], to_island(0, d)) for d in steps]
    zl_part = [role(zl_out.at[z_rows(d)], zl_in.at[d - 1], to_island(d, 0)) for d in steps]
    zl_sum = [role(total_delta.at[my_part], total_delta.at[my_part], to_island(d, 0)) for d in steps]
    y_sum = [role(total_delta.at[mine], total_delta.at[mine], to_island(0, d)) for d in steps]

    base = counter[0]

    def pair(zz, dx):
        return remote(base + zz * 4 + dx, p_out.at[zz, dx], p_in.at[zz, dx], other)

    for n in range(2):
        for m in range(2):
            ag_right[0, 2 * n + m].start()
            ag_left[0, 2 * n + 1 - m].start()
    for n in range(4):
        ag_z[n].start()
    ag_other[0, 0].start()

    load_lev.wait()
    load_scales.wait()
    by_block = scales[...]
    by_row = jnp.transpose(jnp.concatenate([by_block, by_block], axis=0))
    for b in range(KV // BLOCK):
        cols = pl.ds(b * BLOCK, BLOCK)
        lev[:, cols] = (lev[:, cols].astype(f32) * by_row[:, b : b + 1]).astype(bf16)
    for copy in y_part:
        copy.start()

    def normalize(first):
        def body(n, carry):
            rows = pl.ds(pl.multiple_of(first + n * 16, 16), 16)
            total = jnp.zeros((16, 128), f32)
            for k in range(D // 128):
                v = tok[rows, k * 128 : (k + 1) * 128].astype(f32)
                total += v * v
            spread = jnp.sum(total, axis=1, keepdims=True) / D
            inv = lax.rsqrt(spread + norm_eps)
            for k in range(D // 128):
                cols = pl.ds(k * 128, 128)
                v = tok[rows, cols].astype(f32)
                tok[rows, cols] = (v * inv * gain[:, cols]).astype(bf16)
            return carry

        lax.fori_loop(0, CHUNK // 16, body, 0)

    def relay(zz, n):
        (ag_right if n % 2 == 0 else ag_left)[zz, n].wait_recv()
        ag_relay[zz, n].start()

    load_gain.wait()
    for n in range(ROWS // CHUNK):
        loads[n].wait()
        normalize(n * CHUNK)
        if n == 3:
            relay(0, 0)
            relay(0, 1)
    relay(0, 2)
    relay(0, 3)

    def columns(dz, dx, dc):
        return pl.ds(pl.multiple_of(fs(dz, dx, dc) * ROWS, ROWS), ROWS)

    def gradient(dz, dx, dc):
        return lax.dot_general(
            tok[:, columns(dz, dx, dc)],
            cot[...],
            (((0,), (0,)), ((), ())),
            preferred_element_type=f32,
        )

    def give_gradients(zz):
        def give(n, carry):
            dx = (2 + n) % 4
            p_out[zz, dx] = gradient(zz, dx, 1).astype(bf16)
            pair(zz, dx).start()
            return carry

        lax.fori_loop(0, 4, give, 0)

    def keep_gradients(zz, first, last):
        def keep(n, carry):
            dx = (2 + n) % 4
            pair(zz, dx).wait_recv()
            q[zz, dx] = (gradient(zz, dx, 0) + p_in[zz, dx].astype(f32)).astype(bf16)
            return carry

        lax.fori_loop(first, last, keep, 0)

    def scatter_opposite(zz):
        for n in range(2):
            opp_right[zz, n].start()
            opp_left[zz, n].start()

    def scatter_direct(zz):
        dir_right[zz].start()
        dir_left[zz].start()

    def scatter_sums(zz):
        for n in range(2):
            part, upper, lower = quarter(n), quarter(n), quarter(2 + n)
            opp_right[zz, n].wait_recv()
            q[zz, 1, lower] = (q[zz, 1, lower].astype(f32) + r_b[zz, part].astype(f32)).astype(bf16)
            sum_right[zz, n].start()
            opp_left[zz, n].wait_recv()
            q[zz, 3, upper] = (q[zz, 3, upper].astype(f32) + r_a[zz, part].astype(f32)).astype(bf16)
            sum_left[zz, n].start()

    def key_pair(zz, dx, first=False):
        ag_other[zz, dx].wait_recv()

        def body(dc, carry):
            acc[...] += jnp.dot(
                tok[:, columns(zz, dx, dc)], wg[zz, dx, dc], preferred_element_type=f32
            )
            return carry

        if first:
            acc[...] = jnp.zeros_like(acc)
        lax.fori_loop(0, 2, body, 0)

    def share_neighbours(zz):
        for n in (1, 3):
            ag_right[zz, n].wait_recv()
        ag_other[zz, 3].start()
        for n in (0, 2):
            ag_left[zz, n].wait_recv()
        ag_other[zz, 1].start()

    def share_opposite(zz):
        for n in range(4):
            ag_relay[zz, n].wait_recv()
        ag_other[zz, 2].start()

    for copy in y_part:
        copy.wait_recv()
    part = lev[mine].astype(f32)
    for d in range(3):
        part += y_in[d].astype(f32)
    zl_out[...] = part.astype(bf16)
    for copy in zl_part:
        copy.start()

    load_cot.wait()
    give_gradients(1)
    keep_gradients(1, 0, 1)
    scatter_opposite(1)
    keep_gradients(1, 1, 4)
    scatter_direct(1)
    share_neighbours(0)

    for copy in zl_part:
        copy.wait_recv()
    part = zl_out[z_rows(0)].astype(f32)
    for d in range(3):
        part += zl_in[d].astype(f32)
    total_delta[my_part] = part.astype(bf16)
    for copy in zl_sum:
        copy.start()

    key_pair(0, 0, first=True)
    give_gradients(0)
    scatter_sums(1)
    share_opposite(0)
    keep_gradients(0, 0, 4)
    for copy in zl_sum:
        copy.wait_recv()
    for copy in y_sum:
        copy.start()
    key_pair(0, 3)
    key_pair(0, 1)

    dir_right[1].wait_recv()
    dir_left[1].wait_recv()
    for n in range(4):
        ag_z[n].wait_recv()

    def send_across(n):
        rows = quarter(n)
        total = q[1, 0, rows].astype(f32) + from_m[1, rows].astype(f32)
        z_out[rows] = (total + from_p[1, rows].astype(f32)).astype(bf16)
        z_send[n].start()

    for n in range(2):
        sum_left[1, n].wait_recv()
        send_across(n)
        sum_right[1, n].wait_recv()
        send_across(2 + n)
        if n == 0:
            for m in range(2):
                for k in range(2):
                    ag_right[1, 2 * m + k].start()
                    ag_left[1, 2 * m + 1 - k].start()
            ag_other[1, 0].start()

    key_pair(0, 2)
    relay(1, 0)
    relay(1, 1)

    load_ow.wait()
    load_mom.wait()
    for copy in y_sum:
        copy.wait_recv()

    def outer(n, carry):
        rows = pl.ds(pl.multiple_of(n * PART, PART), PART)
        mean = total_delta[rows].astype(f32) / islands
        momentum = keep_rate * mom_out[rows] + mean
        mom_out[rows] = momentum
        ow_out[rows] = ow_out[rows] - outer_rate * (mean + keep_rate * momentum)
        return carry

    lax.fori_loop(0, ROWS // PART, outer, 0)

    key_pair(1, 0)
    relay(1, 2)
    relay(1, 3)
    scatter_opposite(0)
    scatter_direct(0)
    share_neighbours(1)
    key_pair(1, 3)
    key_pair(1, 1)
    scatter_sums(0)
    share_opposite(1)
    key_pair(1, 2)
    keys_out[...] = acc[...].astype(bf16)

    for n in range(4):
        z_send[n].wait_recv()
    dir_right[0].wait_recv()
    dir_left[0].wait_recv()

    def finish(n):
        rows = quarter(n)
        total = q[0, 0, rows].astype(f32) + z_in[rows].astype(f32)
        total += from_m[0, rows].astype(f32) + from_p[0, rows].astype(f32)
        inner = wf[rows] - step_scale * total
        merged_out[rows] = mix_share * inner + (1.0 - mix_share) * ow_out[rows]

    for n in range(2):
        sum_left[0, n].wait_recv()
        finish(n)
        sum_right[0, n].wait_recv()
        finish(2 + n)
    for copy in started:
        copy.wait_send()

    def drain(n, carry):
        pair(n // 4, n % 4).wait_send()
        return carry

    lax.fori_loop(0, 8, drain, 0)


def write(keys, merged, weights, momentum, keys_hbm, merged_hbm, weights_hbm, momentum_hbm, sem):
    pairs = ((merged, merged_hbm), (weights, weights_hbm), (momentum, momentum_hbm), (keys, keys_hbm))
    copies = [pltpu.make_async_copy(a, b, sem.at[n]) for n, (a, b) in enumerate(pairs)]
    for copy in copies:
        copy.start()
    for copy in copies:
        copy.wait()


N_ROLES = 160


def on_device(
    tokens_in,
    norm_gain,
    local_weights,
    cotangent,
    delta_levels,
    block_scales,
    outer_weights_in,
    momentum_in,
):
    features = tokens_in.shape[-1]
    groups = lax.axis_size("fsdp")
    islands = lax.axis_size("island")
    tokens = tokens_in[0].reshape(-1, features)
    tangent = cotangent[0].reshape(-1, cotangent.shape[-1])
    local_rows = tokens.shape[0]
    step_scale = inner_rate / math.sqrt(features) / math.sqrt(local_rows * groups)

    hbm = pl.BlockSpec(memory_space=pltpu.HBM)
    vmem = pl.BlockSpec(memory_space=pltpu.VMEM)
    shapes = (
        jax.ShapeDtypeStruct((ROWS, KV), bf16),
        jax.ShapeDtypeStruct((ROWS, KV), f32),
        jax.ShapeDtypeStruct((ROWS, KV), f32),
        jax.ShapeDtypeStruct((ROWS, KV), f32),
    )
    results = pl.pallas_call(
        functools.partial(kernel, step_scale, islands),
        out_shape=tuple(pltpu.VMEM(s.shape, s.dtype) for s in shapes),
        in_specs=[hbm] * 8,
        out_specs=(vmem,) * 4,
        scratch_shapes=[
            pltpu.VMEM((ROWS, D), bf16),
            pltpu.VMEM((1, D), f32),
            pltpu.VMEM((ROWS, KV), f32),
            pltpu.VMEM((ROWS, KV), bf16),
            pltpu.VMEM((ROWS, KV), bf16),
            pltpu.VMEM((KV // BLOCK, ROWS), f32),
            pltpu.VMEM((2, 4, 2, ROWS, KV), bf16),
            pltpu.VMEM((ROWS, KV), f32),
            pltpu.VMEM((2, 4, ROWS, KV), bf16),
            pltpu.VMEM((2, 4, ROWS, KV), bf16),
            pltpu.VMEM((2, 4, ROWS, KV), bf16),
            pltpu.VMEM((2, HALF, KV), bf16),
            pltpu.VMEM((2, HALF, KV), bf16),
            pltpu.VMEM((2, ROWS, KV), bf16),
            pltpu.VMEM((2, ROWS, KV), bf16),
            pltpu.VMEM((ROWS, KV), bf16),
            pltpu.VMEM((ROWS, KV), bf16),
            pltpu.VMEM((3, QUARTER, KV), bf16),
            pltpu.VMEM((QUARTER, KV), bf16),
            pltpu.VMEM((3, PART, KV), bf16),
            pltpu.VMEM((ROWS, KV), bf16),
            pltpu.SemaphoreType.DMA((7 + ROWS // CHUNK,)),
            pltpu.SemaphoreType.DMA((N_ROLES,)),
            pltpu.SemaphoreType.DMA((N_ROLES,)),
        ],
        compiler_params=pltpu.CompilerParams(
            collective_id=0, has_side_effects=True, vmem_limit_bytes=56 * 2**20
        ),
        cost_estimate=pl.CostEstimate(
            flops=4 * ROWS * D * KV, bytes_accessed=14 * 2**20, transcendentals=ROWS
        ),
    )(
        tokens,
        norm_gain.reshape(1, -1),
        local_weights[0],
        tangent,
        delta_levels[0],
        block_scales[0].T,
        outer_weights_in,
        momentum_in,
    )
    keys, merged, weights_new, momentum_new = pl.pallas_call(
        write,
        out_shape=shapes,
        in_specs=[vmem] * 4,
        out_specs=(hbm,) * 4,
        scratch_shapes=[pltpu.SemaphoreType.DMA((4,))],
        compiler_params=pltpu.CompilerParams(vmem_limit_bytes=2**20),
    )(*results)
    return (keys.reshape(cotangent.shape), merged[None], weights_new, momentum_new)


def solution(mesh):
    in_specs = (
        P("island", None, "fsdp", None),
        P(),
        P("island", "fsdp", None),
        P("island", None, "fsdp", None),
        P("island", "fsdp", None),
        P("island", "fsdp", None),
        P("fsdp", None),
        P("fsdp", None),
    )
    out_specs = (
        P("island", None, "fsdp", None),
        P("island", "fsdp", None),
        P("fsdp", None),
        P("fsdp", None),
    )
    return jax.shard_map(
        on_device, mesh=mesh, in_specs=in_specs, out_specs=out_specs, check_vma=False
    )
```

time: 94.2 us -> 86.3 us (0.916); the launches traced: 92.9 us -> 86.2 us
  local copies, waits for them, and re-layouts: 4.47 us -> 0 us
  other arithmetic: 2.07 us -> 0 us
    unnamed x12 -> x0, local copies, waits for them, and re-layouts: 4.47 us -> none
    broadcast_in_dim x1 -> x0, other arithmetic: 2.07 us -> none  [on_device(): merged[None]]
    pallas_call x1 -> x2, Pallas kernels: 85.6 us -> 85.5 us  [the longest x1 83.7 us: on_device(): pl.pallas_call(functools.partial(kernel, step_scale, islands), out_shape=...]
where the time goes in v2:
time: 86.3 us; the launch traced here: 86.2 us
  Pallas kernels  85.5 us (99%)
    pallas_call x1, Pallas kernels, on_device(): pl.pallas_call(functools.partial(kernel, step_scale, islands), out_shape=...  83.7 us
    pallas_call x1, Pallas kernels, on_device(): pl.pallas_call(write, out_shape=shapes, in_specs=[vmem] * 4, out_specs=(h...  1.87 us

profile of v2, /device:TPU:1, one launch (start us, length us, event | category | flops | bytes accessed | tf_op | source)
XLA Modules:
  0.0 86.2 jit_solution(12990352645248473316)
XLA Ops:
  0.6 83.7 %shard_map.111 = (bf16[512,512]{1,0:T(8,128)(2,1)S(1)}, f32[512,512]{1,0:T(8,128)S(1)}, f32[512,512]{1,0:T(8,128)S(1)}, f32[512,512]{1,0:T(8,128)S(1)}) custom-call(bf16[512,8192]{1,0:T(8,128)(2,1)} %bitcast.10, f32[1,8192]{1,0:T(1,128)} %bitcast.16, f32[512,512]{1,0:T(8,128)} %bitcast.11, bf16[512,512]{1,0:T(8,128)(2,1)} %bitcast.13, ...), custom_call_target="tpu_custom_call" | custom-call | flops 8589934592 | bytes 14680064 | tf_op jit(solution)/shard_map/pallas_call | solution.py:473
  84.3 1.9 %shard_map.112 = (bf16[512,512]{1,0:T(8,128)(2,1)}, f32[512,512]{1,0:T(8,128)}, f32[512,512]{1,0:T(8,128)}, f32[512,512]{1,0:T(8,128)}) custom-call(bf16[512,512]{1,0:T(8,128)(2,1)S(1)} %get-tuple-element.12.keys, f32[512,512]{1,0:T(8,128)S(1)} %get-tuple-element.13.merged, f32[512,512]{1,0:T(8,128)S(1)} %get-tuple-element.14.weights, ...), custom_call_target="tpu_custom_call" | custom-call | tf_op jit(solution)/shard_map/pallas_call | solution.py:520

commit v3 on v2

--- a/solution.py
+++ b/solution.py
@@ -18,6 +18,8 @@
 HALF = 256
 QUARTER = 128
 PART = 32
+MEET_AFTER = 1
+RELAY_AFTER = 4
 CHUNK = 64
 
 norm_eps = 1e-05
@@ -70,6 +72,8 @@
     load_sem,
     send_sem,
     recv_sem,
+    near_sem,
+    far_sem,
 ):
     f = lax.axis_index("fsdp")
     i = lax.axis_index("island")
@@ -128,13 +132,30 @@
     load_mom = load(mom_hbm, mom_out)
 
     barrier = pltpu.get_barrier_semaphore()
-    peers = [right, left, across, other]
-    peers += [to_island(0, d) for d in (1, 2, 3)] + [to_island(d, 0) for d in (1, 2, 3)]
-    for peer in peers:
-        pl.semaphore_signal(barrier, inc=1, device_id=peer, device_id_type=MESH)
+
+    def at_core(device, core):
+        return {"fsdp": (device["fsdp"] // 2) * 2 + core, "island": device["island"]}
+
+    near = [right, left]
+    far = [across]
+    far += [to_island(0, d) for d in (1, 2, 3)] + [to_island(d, 0) for d in (1, 2, 3)]
+    pl.semaphore_signal(barrier, inc=1, device_id=other, device_id_type=MESH)
+    for core, group in ((0, near), (1, far)):
+        for peer in group:
+            pl.semaphore_signal(
+                barrier, inc=1, device_id=at_core(peer, core), device_id_type=MESH
+            )
     load_w.wait()
     wg[0, 0, 0] = wf[...].astype(bf16)
-    pl.semaphore_wait(barrier, len(peers))
+
+    @pl.when(c == 0)
+    def _():
+        pl.semaphore_wait(barrier, 1 + 2 * len(near))
+        pl.semaphore_signal(near_sem, inc=1, device_id=other, device_id_type=MESH)
+
+    @pl.when(c == 1)
+    def _():
+        pl.semaphore_wait(near_sem, 1)
 
     def quarter(n):
         return pl.ds(n * QUARTER, QUARTER)
@@ -189,12 +210,12 @@
     def pair(zz, dx):
         return remote(base + zz * 4 + dx, p_out.at[zz, dx], p_in.at[zz, dx], other)
 
-    for n in range(2):
+    def gather_right_left(zz, n):
         for m in range(2):
-            ag_right[0, 2 * n + m].start()
-            ag_left[0, 2 * n + 1 - m].start()
-    for n in range(4):
-        ag_z[n].start()
+            ag_right[zz, 2 * n + m].start()
+            ag_left[zz, 2 * n + 1 - m].start()
+
+    gather_right_left(0, 0)
     ag_other[0, 0].start()
 
     load_lev.wait()
@@ -204,8 +225,6 @@
     for b in range(KV // BLOCK):
         cols = pl.ds(b * BLOCK, BLOCK)
         lev[:, cols] = (lev[:, cols].astype(f32) * by_row[:, b : b + 1]).astype(bf16)
-    for copy in y_part:
-        copy.start()
 
     def normalize(first):
         def body(n, carry):
@@ -228,11 +247,29 @@
         (ag_right if n % 2 == 0 else ag_left)[zz, n].wait_recv()
         ag_relay[zz, n].start()
 
+    def meet_far():
+        @pl.when(c == 1)
+        def _():
+            pl.semaphore_wait(barrier, 1 + 2 * len(far))
+            pl.semaphore_signal(far_sem, inc=1, device_id=other, device_id_type=MESH)
+
+        @pl.when(c == 0)
+        def _():
+            pl.semaphore_wait(far_sem, 1)
+
+        for n in range(2):
+            ag_z[n].start()
+        gather_right_left(0, 1)
+        for copy in y_part:
+            copy.start()
+
     load_gain.wait()
     for n in range(ROWS // CHUNK):
         loads[n].wait()
         normalize(n * CHUNK)
-        if n == 3:
+        if n == MEET_AFTER:
+            meet_far()
+        if n == RELAY_AFTER:
             relay(0, 0)
             relay(0, 1)
     relay(0, 2)
@@ -312,6 +349,9 @@
             ag_relay[zz, n].wait_recv()
         ag_other[zz, 2].start()
 
+    load_cot.wait()
+    give_gradients(1)
+
     for copy in y_part:
         copy.wait_recv()
     part = lev[mine].astype(f32)
@@ -321,13 +361,20 @@
     for copy in zl_part:
         copy.start()
 
-    load_cot.wait()
-    give_gradients(1)
+    for n in (2, 3):
+        ag_z[n].start()
+
     keep_gradients(1, 0, 1)
     scatter_opposite(1)
     keep_gradients(1, 1, 4)
     scatter_direct(1)
     share_neighbours(0)
+
+    key_pair(0, 0, first=True)
+    give_gradients(0)
+    scatter_sums(1)
+    share_opposite(0)
+    keep_gradients(0, 0, 4)
 
     for copy in zl_part:
         copy.wait_recv()
@@ -338,17 +385,13 @@
     for copy in zl_sum:
         copy.start()
 
-    key_pair(0, 0, first=True)
-    give_gradients(0)
-    scatter_sums(1)
-    share_opposite(0)
-    keep_gradients(0, 0, 4)
+    key_pair(0, 3)
+    key_pair(0, 1)
+
     for copy in zl_sum:
         copy.wait_recv()
     for copy in y_sum:
         copy.start()
-    key_pair(0, 3)
-    key_pair(0, 1)
 
     dir_right[1].wait_recv()
     dir_left[1].wait_recv()
@@ -368,29 +411,12 @@
         send_across(2 + n)
         if n == 0:
             for m in range(2):
-                for k in range(2):
-                    ag_right[1, 2 * m + k].start()
-                    ag_left[1, 2 * m + 1 - k].start()
+                gather_right_left(1, m)
             ag_other[1, 0].start()
 
     key_pair(0, 2)
     relay(1, 0)
     relay(1, 1)
-
-    load_ow.wait()
-    load_mom.wait()
-    for copy in y_sum:
-        copy.wait_recv()
-
-    def outer(n, carry):
-        rows = pl.ds(pl.multiple_of(n * PART, PART), PART)
-        mean = total_delta[rows].astype(f32) / islands
-        momentum = keep_rate * mom_out[rows] + mean
-        mom_out[rows] = momentum
-        ow_out[rows] = ow_out[rows] - outer_rate * (mean + keep_rate * momentum)
-        return carry
-
-    lax.fori_loop(0, ROWS // PART, outer, 0)
 
     key_pair(1, 0)
     relay(1, 2)
@@ -401,6 +427,22 @@
     key_pair(1, 3)
     key_pair(1, 1)
     scatter_sums(0)
+
+    load_ow.wait()
+    load_mom.wait()
+    for copy in y_sum:
+        copy.wait_recv()
+
+    def outer(n, carry):
+        rows = pl.ds(pl.multiple_of(n * PART, PART), PART)
+        mean = total_delta[rows].astype(f32) / islands
+        momentum = keep_rate * mom_out[rows] + mean
+        mom_out[rows] = momentum
+        ow_out[rows] = ow_out[rows] - outer_rate * (mean + keep_rate * momentum)
+        return carry
+
+    lax.fori_loop(0, ROWS // PART, outer, 0)
+
     share_opposite(1)
     key_pair(1, 2)
     keys_out[...] = acc[...].astype(bf16)
@@ -500,6 +542,8 @@
             pltpu.SemaphoreType.DMA((7 + ROWS // CHUNK,)),
             pltpu.SemaphoreType.DMA((N_ROLES,)),
             pltpu.SemaphoreType.DMA((N_ROLES,)),
+            pltpu.SemaphoreType.REGULAR,
+            pltpu.SemaphoreType.REGULAR,
         ],
         compiler_params=pltpu.CompilerParams(
             collective_id=0, has_side_effects=True, vmem_limit_bytes=56 * 2**20

time: 86.3 us -> 82.5 us (0.956)
  the two profiles are of different devices: /device:TPU:1 before, /device:TPU:8 now
where the time goes in v3:
time: 82.5 us
  Pallas kernels  81.8 us (99%)
    pallas_call x1, Pallas kernels, on_device(): pl.pallas_call(functools.partial(kernel, step_scale, islands), out_shape=...  79.9 us
    pallas_call x1, Pallas kernels, on_device(): pl.pallas_call(write, out_shape=shapes, in_specs=[vmem] * 4, out_specs=(h...  1.87 us

profile of v3, /device:TPU:8, one launch (start us, length us, event | category | flops | bytes accessed | tf_op | source)
XLA Modules:
  0.0 82.5 jit_solution(16803885719993452693)
XLA Ops:
  0.6 79.9 %shard_map.111 = (bf16[512,512]{1,0:T(8,128)(2,1)S(1)}, f32[512,512]{1,0:T(8,128)S(1)}, f32[512,512]{1,0:T(8,128)S(1)}, f32[512,512]{1,0:T(8,128)S(1)}) custom-call(bf16[512,8192]{1,0:T(8,128)(2,1)} %bitcast.10, f32[1,8192]{1,0:T(1,128)} %bitcast.16, f32[512,512]{1,0:T(8,128)} %bitcast.11, bf16[512,512]{1,0:T(8,128)(2,1)} %bitcast.13, ...), custom_call_target="tpu_custom_call" | custom-call | flops 8589934592 | bytes 14680064 | tf_op jit(solution)/shard_map/pallas_call | solution.py:515
  80.6 1.9 %shard_map.112 = (bf16[512,512]{1,0:T(8,128)(2,1)}, f32[512,512]{1,0:T(8,128)}, f32[512,512]{1,0:T(8,128)}, f32[512,512]{1,0:T(8,128)}) custom-call(bf16[512,512]{1,0:T(8,128)(2,1)S(1)} %get-tuple-element.12.keys, f32[512,512]{1,0:T(8,128)S(1)} %get-tuple-element.13.merged, f32[512,512]{1,0:T(8,128)S(1)} %get-tuple-element.14.weights, ...), custom_call_target="tpu_custom_call" | custom-call | tf_op jit(solution)/shard_map/pallas_call | solution.py:564

commit v4 on v3

--- a/solution.py
+++ b/solution.py
@@ -119,7 +119,30 @@
         copy.start()
         return copy
 
-    load_w = load(w_hbm, wf)
+    load_w = []
+    for n in range(2):
+        rows = pl.ds(n * HALF, HALF)
+        load_w.append(load(w_hbm.at[rows], wf.at[rows]))
+
+    barrier = pltpu.get_barrier_semaphore()
+
+    def at_core(device, core):
+        return {"fsdp": (device["fsdp"] // 2) * 2 + core, "island": device["island"]}
+
+    near = [right, left]
+    far = [across]
+    far += [to_island(0, d) for d in (1, 2, 3)] + [to_island(d, 0) for d in (1, 2, 3)]
+    pl.semaphore_signal(barrier, inc=1, device_id=other, device_id_type=MESH)
+    for core, group in ((0, near), (1, far)):
+        for peer in group:
+            pl.semaphore_signal(
+                barrier, inc=1, device_id=at_core(peer, core), device_id_type=MESH
+            )
+    load_w[0].wait()
+    wg[0, 0, 0, 0:HALF] = wf[0:HALF].astype(bf16)
+    load_w[1].wait()
+    wg[0, 0, 0, HALF:ROWS] = wf[HALF:ROWS].astype(bf16)
+
     load_lev = load(lev_hbm, lev)
     load_scales = load(scales_hbm, scales)
     load_gain = load(gain_hbm, gain)
@@ -130,23 +153,6 @@
     load_cot = load(cot_hbm, cot)
     load_ow = load(ow_hbm, ow_out)
     load_mom = load(mom_hbm, mom_out)
-
-    barrier = pltpu.get_barrier_semaphore()
-
-    def at_core(device, core):
-        return {"fsdp": (device["fsdp"] // 2) * 2 + core, "island": device["island"]}
-
-    near = [right, left]
-    far = [across]
-    far += [to_island(0, d) for d in (1, 2, 3)] + [to_island(d, 0) for d in (1, 2, 3)]
-    pl.semaphore_signal(barrier, inc=1, device_id=other, device_id_type=MESH)
-    for core, group in ((0, near), (1, far)):
-        for peer in group:
-            pl.semaphore_signal(
-                barrier, inc=1, device_id=at_core(peer, core), device_id_type=MESH
-            )
-    load_w.wait()
-    wg[0, 0, 0] = wf[...].astype(bf16)
 
     @pl.when(c == 0)
     def _():
@@ -376,6 +382,26 @@
     share_opposite(0)
     keep_gradients(0, 0, 4)
 
+    key_pair(0, 3)
+    key_pair(0, 1)
+
+    dir_right[1].wait_recv()
+    dir_left[1].wait_recv()
+    for n in range(4):
+        ag_z[n].wait_recv()
+
+    def send_across(n):
+        rows = quarter(n)
+        total = q[1, 0, rows].astype(f32) + from_m[1, rows].astype(f32)
+        z_out[rows] = (total + from_p[1, rows].astype(f32)).astype(bf16)
+        z_send[n].start()
+
+    sum_left[1, 0].wait_recv()
+
+    gather_right_left(1, 0)
+    gather_right_left(1, 1)
+    ag_other[1, 0].start()
+
     for copy in zl_part:
         copy.wait_recv()
     part = zl_out[z_rows(0)].astype(f32)
@@ -385,34 +411,13 @@
     for copy in zl_sum:
         copy.start()
 
-    key_pair(0, 3)
-    key_pair(0, 1)
-
-    for copy in zl_sum:
-        copy.wait_recv()
-    for copy in y_sum:
-        copy.start()
-
-    dir_right[1].wait_recv()
-    dir_left[1].wait_recv()
-    for n in range(4):
-        ag_z[n].wait_recv()
-
-    def send_across(n):
-        rows = quarter(n)
-        total = q[1, 0, rows].astype(f32) + from_m[1, rows].astype(f32)
-        z_out[rows] = (total + from_p[1, rows].astype(f32)).astype(bf16)
-        z_send[n].start()
-
-    for n in range(2):
-        sum_left[1, n].wait_recv()
-        send_across(n)
-        sum_right[1, n].wait_recv()
-        send_across(2 + n)
-        if n == 0:
-            for m in range(2):
-                gather_right_left(1, m)
-            ag_other[1, 0].start()
+    send_across(0)
+    sum_right[1, 0].wait_recv()
+    send_across(2)
+    sum_left[1, 1].wait_recv()
+    send_across(1)
+    sum_right[1, 1].wait_recv()
+    send_across(3)
 
     key_pair(0, 2)
     relay(1, 0)
@@ -428,6 +433,15 @@
     key_pair(1, 1)
     scatter_sums(0)
 
+    for copy in zl_sum:
+        copy.wait_recv()
+    for copy in y_sum:
+        copy.start()
+
+    share_opposite(1)
+    key_pair(1, 2)
+    keys_out[...] = acc[...].astype(bf16)
+
     load_ow.wait()
     load_mom.wait()
     for copy in y_sum:
@@ -442,10 +456,6 @@
         return carry
 
     lax.fori_loop(0, ROWS // PART, outer, 0)
-
-    share_opposite(1)
-    key_pair(1, 2)
-    keys_out[...] = acc[...].astype(bf16)
 
     for n in range(4):
         z_send[n].wait_recv()
@@ -539,7 +549,7 @@
             pltpu.VMEM((QUARTER, KV), bf16),
             pltpu.VMEM((3, PART, KV), bf16),
             pltpu.VMEM((ROWS, KV), bf16),
-            pltpu.SemaphoreType.DMA((7 + ROWS // CHUNK,)),
+            pltpu.SemaphoreType.DMA((8 + ROWS // CHUNK,)),
             pltpu.SemaphoreType.DMA((N_ROLES,)),
             pltpu.SemaphoreType.DMA((N_ROLES,)),
             pltpu.SemaphoreType.REGULAR,

time: 82.5 us -> 80.8 us (0.979)
  the two profiles are of different devices: /device:TPU:8 before, /device:TPU:1 now
where the time goes in v4:
time: 80.8 us; the launch traced here: 80.7 us
  Pallas kernels  80 us (99%)
    pallas_call x1, Pallas kernels, on_device(): pl.pallas_call(functools.partial(kernel, step_scale, islands), out_shape=...  78.2 us
    pallas_call x1, Pallas kernels, on_device(): pl.pallas_call(write, out_shape=shapes, in_specs=[vmem] * 4, out_specs=(h...  1.87 us

profile of v4, /device:TPU:1, one launch (start us, length us, event | category | flops | bytes accessed | tf_op | source)
XLA Modules:
  0.0 80.7 jit_solution(4247859098156592504)
XLA Ops:
  0.6 78.2 %shard_map.111 = (bf16[512,512]{1,0:T(8,128)(2,1)S(1)}, f32[512,512]{1,0:T(8,128)S(1)}, f32[512,512]{1,0:T(8,128)S(1)}, f32[512,512]{1,0:T(8,128)S(1)}) custom-call(bf16[512,8192]{1,0:T(8,128)(2,1)} %bitcast.10, f32[1,8192]{1,0:T(1,128)} %bitcast.16, f32[512,512]{1,0:T(8,128)} %bitcast.11, bf16[512,512]{1,0:T(8,128)(2,1)} %bitcast.13, ...), custom_call_target="tpu_custom_call" | custom-call | flops 8589934592 | bytes 14680064 | tf_op jit(solution)/shard_map/pallas_call | solution.py:525
  78.8 1.9 %shard_map.112 = (bf16[512,512]{1,0:T(8,128)(2,1)}, f32[512,512]{1,0:T(8,128)}, f32[512,512]{1,0:T(8,128)}, f32[512,512]{1,0:T(8,128)}) custom-call(bf16[512,512]{1,0:T(8,128)(2,1)S(1)} %get-tuple-element.12.keys, f32[512,512]{1,0:T(8,128)S(1)} %get-tuple-element.13.merged, f32[512,512]{1,0:T(8,128)S(1)} %get-tuple-element.14.weights, ...), custom_call_target="tpu_custom_call" | custom-call | tf_op jit(solution)/shard_map/pallas_call | solution.py:574

commit v5 on v4

--- a/solution.py
+++ b/solution.py
@@ -358,6 +358,14 @@
     load_cot.wait()
     give_gradients(1)
 
+    for n in (2, 3):
+        ag_z[n].start()
+
+    keep_gradients(1, 0, 1)
+    scatter_opposite(1)
+    keep_gradients(1, 1, 4)
+    scatter_direct(1)
+
     for copy in y_part:
         copy.wait_recv()
     part = lev[mine].astype(f32)
@@ -366,14 +374,6 @@
     zl_out[...] = part.astype(bf16)
     for copy in zl_part:
         copy.start()
-
-    for n in (2, 3):
-        ag_z[n].start()
-
-    keep_gradients(1, 0, 1)
-    scatter_opposite(1)
-    keep_gradients(1, 1, 4)
-    scatter_direct(1)
     share_neighbours(0)
 
     key_pair(0, 0, first=True)

time: 80.8 us -> 80.7 us (level)
  no operation moved by 1% of the time
where the time goes in v5:
time: 80.7 us; the launch traced here: 80.6 us
  Pallas kernels  80 us (99%)
    pallas_call x1, Pallas kernels, on_device(): pl.pallas_call(functools.partial(kernel, step_scale, islands), out_shape=...  78.1 us
    pallas_call x1, Pallas kernels, on_device(): pl.pallas_call(write, out_shape=shapes, in_specs=[vmem] * 4, out_specs=(h...  1.87 us

profile of v5, /device:TPU:1, one launch (start us, length us, event | category | flops | bytes accessed | tf_op | source)
XLA Modules:
  0.0 80.6 jit_solution(16272295185134575642)
XLA Ops:
  0.6 78.1 %shard_map.111 = (bf16[512,512]{1,0:T(8,128)(2,1)S(1)}, f32[512,512]{1,0:T(8,128)S(1)}, f32[512,512]{1,0:T(8,128)S(1)}, f32[512,512]{1,0:T(8,128)S(1)}) custom-call(bf16[512,8192]{1,0:T(8,128)(2,1)} %bitcast.10, f32[1,8192]{1,0:T(1,128)} %bitcast.16, f32[512,512]{1,0:T(8,128)} %bitcast.11, bf16[512,512]{1,0:T(8,128)(2,1)} %bitcast.13, ...), custom_call_target="tpu_custom_call" | custom-call | flops 8589934592 | bytes 14680064 | tf_op jit(solution)/shard_map/pallas_call | solution.py:525
  78.8 1.9 %shard_map.112 = (bf16[512,512]{1,0:T(8,128)(2,1)}, f32[512,512]{1,0:T(8,128)}, f32[512,512]{1,0:T(8,128)}, f32[512,512]{1,0:T(8,128)}) custom-call(bf16[512,512]{1,0:T(8,128)(2,1)S(1)} %get-tuple-element.12.keys, f32[512,512]{1,0:T(8,128)S(1)} %get-tuple-element.13.merged, f32[512,512]{1,0:T(8,128)S(1)} %get-tuple-element.14.weights, ...), custom_call_target="tpu_custom_call" | custom-call | tf_op jit(solution)/shard_map/pallas_call | solution.py:574
